TPU v7x, 32 devices: a whole 2x2x4 slice. The times are simulated.
32 devices in a mesh: rows: 16 (over z, x, core), dirs: 2 (over y).
Axes of the slice: x: 2, y: 2, z: 4, core: 2. Of those that a mesh axis runs over, the one named last changes fastest.
Arguments:
- previous: bfloat16 [24, 32, 128, 512], P('dirs', None, 'rows'), may hold values from -12 to 12
- boundary: float32 [24, 32, 512], P('dirs'), may hold values from -6 to 6
- row_coupling: float32 [24, 128, 512], P('dirs', 'rows'), may hold values from 0 to 1
- cross_gain: float32 [24], P('dirs'), may hold values from 0.5 to 3
- block_inverse: float32 [24, 128, 128], P('dirs'), may hold values from 0 to 1, as said below
- quadrant: int32 [24], P('dirs'), may hold values from 0 to 3
- sea_mask: int32 [128, 512], P('rows'), may hold values from 0 to 1, as said below
- wet_tiles: int32 [128, 4], P('rows'), may hold values 0 or 1
- quad_coef: float32 [32], replicated, may hold values from 0.05 to 0.5
Outputs:
- action: bfloat16 [24, 32, 128, 512], P('dirs', None, 'rows')
Inputs may be any that keep to these rules, and one draw needn't show every extreme that they name: `sea_mask`: in each row the land cells, if any, are the last ones, from a coastline column to the end of the row. block_inverse[d] is the inverse of the 128 x 128 lower bidiagonal matrix with 1 + cross_gain[d] on its diagonal and -cross_gain[d] just below it.
All inputs are finite; a program needn't handle non-finite values. No bound on the sum of `wet_tiles` on one device may be relied on, other than what follows from the above.
Results may differ from a plain program's by a relative error of at most 0.0027.
Values may be sent and summed in bfloat16 or wider, within the bound.
A program may use at most 128 MiB of HBM per device.

v0:
```python
import jax
import jax.numpy as jnp
from jax import lax
from jax.sharding import PartitionSpec as P

SHIFT = 2


highest = lax.Precision.HIGHEST


def compose(preceding_part, following_part):
    return (
        following_part[0] * preceding_part[0],
        following_part[0] * preceding_part[1] + following_part[1],
    )


def higher_band(field):
    return jnp.concatenate([field[:, 1:], jnp.zeros_like(field[:, :1])], axis=1)


def lower_band(field):
    return jnp.concatenate([jnp.zeros_like(field[:, :1]), field[:, :-1]], axis=1)


def quad_terms(center, onward, against, coefficients):
    nonlinear = center * center * (onward + against) - 2.0 * center * onward * against
    return coefficients[None, :, None, None] * nonlinear


def full_source(spectra, coefficients):
    energy = spectra.astype(jnp.float32)
    onward = higher_band(jnp.roll(energy, -SHIFT, axis=0))
    against = lower_band(jnp.roll(energy, SHIFT, axis=0))
    return quad_terms(energy, onward, against, coefficients)


def on_device(
    previous,
    boundary,
    row_coupling,
    cross_gain,
    block_inverse,
    quadrant,
    sea_mask,
    wet_tiles,
    quad_coef,
):
    dir_dev, band_count, row_count, column_count = previous.shape
    block_size = block_inverse.shape[-1]
    sea_cells = sea_mask.astype(jnp.float32)
    backward = quadrant % 2 == 1
    sideways = quadrant // 2 == 1
    couple = row_coupling * sea_cells[None]
    forcing = sea_cells[None, None] * (1.0 - row_coupling)[:, None] * previous.astype(jnp.float32)
    couple = jnp.where(backward[:, None, None], jnp.flip(couple, 1), couple)
    forcing = jnp.where(backward[:, None, None, None], jnp.flip(forcing, 2), forcing)

    def row_step(carry, member):
        gain_now, value_now = carry
        gain_next = member[0][:, None] * gain_now
        value_next = member[0][:, None] * value_now + member[1]
        return ((gain_next, value_next), (gain_next, value_next))

    start_gain = jnp.ones((dir_dev, 1, column_count), jnp.float32)
    start_value = jnp.zeros((dir_dev, band_count, column_count), jnp.float32)
    last_maps, row_maps = lax.scan(
        row_step,
        (start_gain, start_value),
        (jnp.moveaxis(couple, 1, 0), jnp.moveaxis(forcing, 2, 0)),
    )
    span_gain = jnp.moveaxis(row_maps[0], 0, 2)
    partial_value = jnp.moveaxis(row_maps[1], 0, 2)
    block_gain, block_state = last_maps
    every_gain, every_state = (
        lax.all_gather(block_gain[None], "rows", axis=0, tiled=True),
        lax.all_gather(block_state[None], "rows", axis=0, tiled=True),
    )
    device_count = every_gain.shape[0]
    position = lax.axis_index("rows")
    order_flipping = backward[None, :, None, None]
    ordered_gain = jnp.where(order_flipping, jnp.flip(every_gain, 0), every_gain)
    ordered_state = jnp.where(order_flipping, jnp.flip(every_state, 0), every_state)

    def device_step(carry, member):
        return (compose(carry, member), carry)

    _, before_maps = lax.scan(
        device_step,
        (jnp.ones_like(block_gain), jnp.zeros_like(block_state)),
        (ordered_gain, ordered_state),
    )
    before_gain, before_state = before_maps
    onward_gain = lax.dynamic_index_in_dim(before_gain, position, 0, keepdims=False)
    onward_state = lax.dynamic_index_in_dim(before_state, position, 0, keepdims=False)
    against_gain = lax.dynamic_index_in_dim(
        before_gain, device_count - 1 - position, 0, keepdims=False
    )
    against_state = lax.dynamic_index_in_dim(
        before_state, device_count - 1 - position, 0, keepdims=False
    )
    inflow_gain = jnp.where(backward[:, None, None], against_gain, onward_gain)
    inflow_state = jnp.where(backward[:, None, None], against_state, onward_state)
    entering = inflow_gain * boundary + inflow_state
    swept_rows = partial_value + span_gain * entering[:, :, None, :]
    swept_rows = jnp.where(backward[:, None, None, None], jnp.flip(swept_rows, 2), swept_rows)
    flipped = jnp.where(sideways[:, None, None, None], jnp.flip(swept_rows, 3), swept_rows)
    blocks = flipped.reshape(dir_dev, band_count, row_count, column_count // block_size, block_size)
    solved = jnp.einsum(
        "dij,dfrkj->dfrki",
        block_inverse,
        blocks,
        precision=highest,
        preferred_element_type=jnp.float32,
    )
    first_column = block_inverse[:, :, 0][:, None, None, :]
    gain_column = cross_gain[:, None, None, None]
    pieces = [solved[:, :, :, 0]]
    for section in range(1, column_count // block_size):
        pieces.append(solved[:, :, :, section] + gain_column * pieces[-1][..., -1:] * first_column)
    settled = jnp.stack(pieces, 3).reshape(dir_dev, band_count, row_count, column_count)
    settled = (
        jnp.where(sideways[:, None, None, None], jnp.flip(settled, 3), settled)
        * sea_cells[None, None]
    )
    rounded = lax.optimization_barrier(settled.astype(jnp.bfloat16))
    gained = full_source(
        lax.all_to_all(rounded, "dirs", split_axis=2, concat_axis=0, tiled=True), quad_coef
    ).astype(jnp.bfloat16)
    returned = lax.all_to_all(gained, "dirs", split_axis=0, concat_axis=2, tiled=True)
    returned = lax.optimization_barrier(returned)
    wet_cells = jnp.repeat(wet_tiles.astype(jnp.float32), block_size, axis=1)
    return (settled + wet_cells[None, None] * returned.astype(jnp.float32)).astype(jnp.bfloat16)


def solution(mesh):
    in_specs = (
        P("dirs", None, "rows", None),
        P("dirs", None, None),
        P("dirs", "rows", None),
        P("dirs"),
        P("dirs", None, None),
        P("dirs"),
        P("rows", None),
        P("rows", None),
        P(),
    )
    out_specs = P("dirs", None, "rows", None)
    return jax.shard_map(
        on_device, mesh=mesh, in_specs=in_specs, out_specs=out_specs, check_vma=False
    )
```

profile of v0, /device:TPU:0, one launch (start us, length us, event | category | flops | bytes accessed | tf_op | source)
XLA Modules:
  0.0 633.3 jit_solution(5337060883751082020)
XLA Ops:
  14.3 11.2 %rev.27 = f32[12,32,8,512]{3,2,1,0:T(8,128)} reverse(f32[12,32,8,512]{3,2,1,0:T(8,128)} %convert_multiply_fusion), dimensions={2} | reverse | bytes 12582912 | tf_op jit(solution)/shard_map/jit(_flip)/rev | solution.py:58
  33.3 173.7 %while.34 = (s32[]{:T(128)}, f32[12,1,512]{2,1,0:T(1,128)S(1)}, f32[12,32,512]{2,1,0:T(8,128)S(1)}, f32[8,12,1,512]{3,0,1,2:T(8,128)S(1)}, f32[8,12,32,512]{3,0,...) while((s32[]{:T(128)}, f32[12,1,512]{2,1,0:T(1,128)S(1)}, ...), condition=%wide.region_1.2_spmd.clone, body=%wide.region_0.1_spmd.clone.sunk | while | flops 602115 | bytes 7299192 | solution.py:68
  38.3 16.7 %dynamic_update_slice.27 = f32[8,12,32,512]{3,0,2,1:T(8,128)} dynamic-update-slice(f32[8,12,32,512]{3,0,2,1:T(8,128)} %get-tuple-element.342, f32[1,12,32,512]{3,0,2,1:T(1,128)S(1)} %copy.159, s32[]{:T(128)} %get-tuple-element.338, s32[]{:T(128)} %constant.78.clone.1..sunk, s32[]{:T(128)} %constant.78.clone.1..sunk, s32[]{:T(128)} %constant.78.clone.1..sunk) | dynamic-update-slice | bytes 1572868 | tf_op jit(solution)/shard_map/while/body/jit(dynamic_update_index_in_dim)/dynamic_update_slice | solution.py:68
  60.0 16.7 %dynamic_update_slice.27 = f32[8,12,32,512]{3,0,2,1:T(8,128)} dynamic-update-slice(f32[8,12,32,512]{3,0,2,1:T(8,128)} %get-tuple-element.342, f32[1,12,32,512]{3,0,2,1:T(1,128)S(1)} %copy.159, s32[]{:T(128)} %get-tuple-element.338, s32[]{:T(128)} %constant.78.clone.1..sunk, s32[]{:T(128)} %constant.78.clone.1..sunk, s32[]{:T(128)} %constant.78.clone.1..sunk) | dynamic-update-slice | bytes 1572868 | tf_op jit(solution)/shard_map/while/body/jit(dynamic_update_index_in_dim)/dynamic_update_slice | solution.py:68
  81.7 16.7 %dynamic_update_slice.27 = f32[8,12,32,512]{3,0,2,1:T(8,128)} dynamic-update-slice(f32[8,12,32,512]{3,0,2,1:T(8,128)} %get-tuple-element.342, f32[1,12,32,512]{3,0,2,1:T(1,128)S(1)} %copy.159, s32[]{:T(128)} %get-tuple-element.338, s32[]{:T(128)} %constant.78.clone.1..sunk, s32[]{:T(128)} %constant.78.clone.1..sunk, s32[]{:T(128)} %constant.78.clone.1..sunk) | dynamic-update-slice | bytes 1572868 | tf_op jit(solution)/shard_map/while/body/jit(dynamic_update_index_in_dim)/dynamic_update_slice | solution.py:68
  103.4 16.7 %dynamic_update_slice.27 = f32[8,12,32,512]{3,0,2,1:T(8,128)} dynamic-update-slice(f32[8,12,32,512]{3,0,2,1:T(8,128)} %get-tuple-element.342, f32[1,12,32,512]{3,0,2,1:T(1,128)S(1)} %copy.159, s32[]{:T(128)} %get-tuple-element.338, s32[]{:T(128)} %constant.78.clone.1..sunk, s32[]{:T(128)} %constant.78.clone.1..sunk, s32[]{:T(128)} %constant.78.clone.1..sunk) | dynamic-update-slice | bytes 1572868 | tf_op jit(solution)/shard_map/while/body/jit(dynamic_update_index_in_dim)/dynamic_update_slice | solution.py:68
  125.1 16.7 %dynamic_update_slice.27 = f32[8,12,32,512]{3,0,2,1:T(8,128)} dynamic-update-slice(f32[8,12,32,512]{3,0,2,1:T(8,128)} %get-tuple-element.342, f32[1,12,32,512]{3,0,2,1:T(1,128)S(1)} %copy.159, s32[]{:T(128)} %get-tuple-element.338, s32[]{:T(128)} %constant.78.clone.1..sunk, s32[]{:T(128)} %constant.78.clone.1..sunk, s32[]{:T(128)} %constant.78.clone.1..sunk) | dynamic-update-slice | bytes 1572868 | tf_op jit(solution)/shard_map/while/body/jit(dynamic_update_index_in_dim)/dynamic_update_slice | solution.py:68
  146.8 16.7 %dynamic_update_slice.27 = f32[8,12,32,512]{3,0,2,1:T(8,128)} dynamic-update-slice(f32[8,12,32,512]{3,0,2,1:T(8,128)} %get-tuple-element.342, f32[1,12,32,512]{3,0,2,1:T(1,128)S(1)} %copy.159, s32[]{:T(128)} %get-tuple-element.338, s32[]{:T(128)} %constant.78.clone.1..sunk, s32[]{:T(128)} %constant.78.clone.1..sunk, s32[]{:T(128)} %constant.78.clone.1..sunk) | dynamic-update-slice | bytes 1572868 | tf_op jit(solution)/shard_map/while/body/jit(dynamic_update_index_in_dim)/dynamic_update_slice | solution.py:68
  168.5 16.7 %dynamic_update_slice.27 = f32[8,12,32,512]{3,0,2,1:T(8,128)} dynamic-update-slice(f32[8,12,32,512]{3,0,2,1:T(8,128)} %get-tuple-element.342, f32[1,12,32,512]{3,0,2,1:T(1,128)S(1)} %copy.159, s32[]{:T(128)} %get-tuple-element.338, s32[]{:T(128)} %constant.78.clone.1..sunk, s32[]{:T(128)} %constant.78.clone.1..sunk, s32[]{:T(128)} %constant.78.clone.1..sunk) | dynamic-update-slice | bytes 1572868 | tf_op jit(solution)/shard_map/while/body/jit(dynamic_update_index_in_dim)/dynamic_update_slice | solution.py:68
  190.3 16.7 %dynamic_update_slice.27 = f32[8,12,32,512]{3,0,2,1:T(8,128)} dynamic-update-slice(f32[8,12,32,512]{3,0,2,1:T(8,128)} %get-tuple-element.342, f32[1,12,32,512]{3,0,2,1:T(1,128)S(1)} %copy.159, s32[]{:T(128)} %get-tuple-element.338, s32[]{:T(128)} %constant.78.clone.1..sunk, s32[]{:T(128)} %constant.78.clone.1..sunk, s32[]{:T(128)} %constant.78.clone.1..sunk) | dynamic-update-slice | bytes 1572868 | tf_op jit(solution)/shard_map/while/body/jit(dynamic_update_index_in_dim)/dynamic_update_slice | solution.py:68
  208.4 25.4 %all-gather = f32[192,1,512]{2,1,0:T(1,128)S(1)} all-gather(f32[12,1,512]{2,1,0:T(1,128)S(1)} %get-tuple-element.85), channel_id=2, replica_groups=mesh['rows'=16,'dirs'=2] {'rows'}, dimensions={0}, use_global_device_ids=true | all-gather | bytes 417792 | tf_op jit(solution)/shard_map/all_gather | solution.py:77
  234.9 77.5 %all-gather.4.cloned.1.call-done = f32[192,32,512]{2,1,0:T(8,128)} async-done(((f32[12,32,512]{2,1,0:T(8,128)}), f32[192,32,512]{2,1,0:T(8,128)}) %all-gather.4.cloned.1.call-update) | async-done | bytes 12582928 | tf_op jit(solution)/shard_map/all_gather | solution.py:78
  312.4 17.5 %reverse_select_fusion = f32[16,12,32,512]{3,2,1,0:T(8,128)} fusion(f32[16,12,32,512]{3,2,1,0:T(8,128)} %bitcast.110, pred[12]{0:T(512)(128)(4,1)S(1)} %get-tuple-element.234), kind=kLoop, calls=%fused_computation.15 | loop fusion | flops 3145728 | bytes 25165836 | tf_op jit(solution)/shard_map/jit(_where)/select_n | solution.py:84
  329.9 61.8 %while.35 = (s32[]{:T(128)}, f32[12,1,512]{2,1,0:T(1,128)S(1)}, f32[12,32,512]{2,1,0:T(8,128)S(1)}, f32[16,12,1,512]{3,2,1,0:T(1,128)}, f32[16,12,32,512]{3,2,1,...) while((s32[]{:T(128)}, f32[12,1,512]{2,1,0:T(1,128)S(1)}, ...), condition=%wide.region_3.4_spmd.clone, body=%wide.region_2.3_spmd.clone.sunk | while | flops 804867 | bytes 4154482 | solution.py:89
  400.8 11.2 %rev.30 = f32[12,32,8,512]{3,2,1,0:T(8,128)} reverse(f32[12,32,8,512]{3,2,1,0:T(8,128)} %bitcast_add_fusion.1), dimensions={2} | reverse | bytes 12582912 | tf_op jit(solution)/shard_map/jit(_flip)/rev | solution.py:107
  412.0 9.4 %broadcast_select_fusion.2 = f32[12,32,8,512]{3,2,1,0:T(8,128)} fusion(f32[12,32,8,512]{3,2,1,0:T(8,128)} %rev.30, pred[12]{0:T(512)(128)(4,1)S(1)} %get-tuple-element.234, f32[12,32,512]{2,1,0:T(8,128)S(1)} %fusion.8, f32[12,8,512]{2,1,0:T(8,128)S(1)} %bitcast.119, f32[8,12,32,512]{3,0,2,1:T(8,128)} %get-tuple-element.83), kind=kLoop, calls=%fused_computation.34 | loop fusion | flops 4718592 | bytes 19857420 | tf_op jit(solution)/shard_map/jit(_where)/select_n | solution.py:107
  421.5 12.5 %rev.31 = f32[12,32,8,512]{3,2,1,0:T(8,128)} reverse(f32[12,32,8,512]{3,2,1,0:T(8,128)} %broadcast_select_fusion.2), dimensions={3} | reverse | bytes 12582912 | tf_op jit(solution)/shard_map/jit(_flip)/rev | solution.py:108
  433.9 8.6 %fusion.2 = f32[12,32,8,4,128]{4,2,3,1,0:T(8,128)S(1)} fusion(f32[12,32,8,512]{3,2,1,0:T(8,128)} %rev.31, f32[12,32,8,512]{3,2,1,0:T(8,128)} %broadcast_select_fusion.2, pred[12]{0:T(512)(128)(4,1)S(1)} %get-tuple-element.233, f32[12,128,128]{2,1,0:T(8,128)S(1)} %copy-done.1), kind=kOutput, calls=%fused_computation.22 | convolution fusion | flops 2417491968 | bytes 19660812 | tf_op jit(solution)/shard_map/dij,dfrkj->dfrki/dot_general | solution.py:110
  466.7 14.3 %multiply_add_fusion.2 = (f32[12,32,8,1,128]{1,2,4,0,3:T(8,128)}, f32[12,32,8,1,128]{1,2,4,0,3:T(8,128)}, f32[12,32,8,1,128]{1,2,4,0,3:T(8,128)}) fusion(f32[12,32,8,1,128]{1,2,4,0,3:T(8,128)} %copy.137, f32[12,128]{1,0:T(8,128)S(1)} %bitcast.121, f32[12,32,8]{1,2,0:T(8,128)S(1)} %fusion.13, f32[12,32,8,1,128]{1,2,4,0,3:T(8,128)} %copy.139, ...), kind=kLoop, calls=%fused_computation.30 | loop fusion | flops 2359296 | bytes 9480192 | tf_op jit(solution)/shard_map/add | solution.py:121
  502.0 12.5 %rev.32 = f32[12,32,8,512]{3,2,1,0:T(8,128)} reverse(f32[12,32,8,512]{3,2,1,0:T(8,128)} %maximum_bitcast_fusion), dimensions={3} | reverse | bytes 12582912 | tf_op jit(solution)/shard_map/jit(_flip)/rev | solution.py:124
  520.3 39.4 %all_to_all.27 = bf16[12,32,8,512]{3,1,0,2:T(8,128)(2,1)S(1)} all-to-all(bf16[12,32,8,512]{3,1,0,2:T(8,128)(2,1)S(1)} %copy.121), channel_id=1, replica_groups=mesh['rows'=16,'dirs'=2] {'dirs'}, dimensions={2} | all-to-all | bytes 6291456 | tf_op jit(solution)/shard_map/all_to_all | solution.py:129
  567.7 7.7 %multiply_convert_fusion = bf16[24,32,4,512]{3,1,2,0:T(8,128)(2,1)} fusion(f32[2,32,4,512]{3,1,2,0:T(8,128)S(1)} %get-tuple-element.219, f32[22,32,4,512]{3,1,2,0:T(8,128)} %get-tuple-element.221, f32[22,32,4,512]{3,1,2,0:T(8,128)} %get-tuple-element.220, f32[2,32,4,512]{3,1,2,0:T(8,128)S(1)} %get-tuple-element.218, f32[32]{0:T(128)S(1)} %copy-done.5, ...), kind=kLoop, calls=%fused_computation.26 | loop fusion | flops 26738688 | bytes 22020224 | tf_op jit(solution)/shard_map/convert_element_type | solution.py:130
  580.8 35.9 %all-to-all-done.1 = bf16[24,32,4,512]{3,1,2,0:T(8,128)(2,1)} async-done(((bf16[24,32,4,512]{3,1,2,0:T(8,128)(2,1)}), bf16[24,32,4,512]{3,1,2,0:T(8,128)(2,1)}, u32[]{:S(2)}, u32[]{:S(2)}) %all-to-all-start.1) | async-done | bytes 3145760 | tf_op jit(solution)/shard_map/all_to_all | solution.py:131
  618.8 7.6 %add_convert_fusion = bf16[12,32,8,512]{3,2,1,0:T(8,128)(2,1)} fusion(bf16[12,32,8,512]{3,1,2,0:T(8,128)(2,1)S(1)} %bitcast.111, f32[8,512]{1,0:T(8,128)S(1)} %broadcast_bitcast_fusion, f32[8,512]{1,0:T(8,128)S(1)} %convert_element_type.33, f32[12,32,8,512]{3,2,1,0:T(8,128)} %rev.32, pred[12]{0:T(512)(128)(4,1)S(1)} %get-tuple-element.233, ...), kind=kLoop, calls=%fused_computation.25 | loop fusion | flops 14155776 | bytes 18907148 | tf_op jit(solution)/shard_map/convert_element_type | solution.py:134
  (187 shorter events, 194.9 us)
Async XLA Ops:
  6.5 305.9 %all-gather.4.cloned.1.call-start = ((), (), s32[]{:S(2)}) async-start(), calls=%async_computation.2 | async-start | bytes 13369344 | tf_op jit(solution)/shard_map/all_gather | solution.py:78
  33.3 174.7 %copy-start.1 = (f32[12,128,128]{2,1,0:T(8,128)S(1)}, f32[12,128,128]{2,1,0:T(8,128)}, u32[]{:S(2)}) copy-start(f32[12,128,128]{2,1,0:T(8,128)} %param.17) | copy-start | bytes 2359300
  207.1 0.9 copy-start
  329.9 62.6 %copy-start.2 = (f32[12,32,512]{2,1,0:T(8,128)S(1)}, f32[12,32,512]{2,1,0:T(8,128)}, u32[]{:S(2)}) copy-start(f32[12,32,512]{2,1,0:T(8,128)} %param.14) | copy-start | bytes 2359300
  454.0 10.1 %copy-start.3 = (f32[12]{0:T(128)S(1)}, f32[12]{0:T(128)}, u32[]{:S(2)}) copy-start(f32[12]{0:T(128)} %param.16) | copy-start | bytes 148
  561.8 5.8 copy-start.5
  575.3 5.3 copy-start.4
  575.3 41.4 %all-to-all-start.1 = ((bf16[24,32,4,512]{3,1,2,0:T(8,128)(2,1)}), bf16[24,32,4,512]{3,1,2,0:T(8,128)(2,1)}, u32[]{:S(2)}, u32[]{:S(2)}) async-start(bf16[24,32,4,512]{3,1,2,0:T(8,128)(2,1)} %multiply_convert_fusion), calls=%async_computation.1 | async-start | bytes 6291456 | tf_op jit(solution)/shard_map/all_to_all | solution.py:131
Sparse Core Ops, SparseCore 0:
  208.1 104.2 all-gather.3
where the time goes:
time: 641 us; the launch traced here: 633 us
  local copies, waits for them, and re-layouts  268 us (42%)
  other arithmetic  159 us (25%)
  waiting for transfers between devices  113 us (18%)
  blocking collectives  64.8 us (10%)
  between operations  13.6 us (2%)
  matrix products  8.55 us (1%)
    dynamic_update_slice x24, local copies, waits for them, and re-layouts, on_device(): lax.scan(row_step, (start_gain, start_value), (jnp.moveaxis(couple, 1, 0)...  141 us
    all_gather x1, waiting for transfers between devices, on_device(): lax.all_gather(block_state[None], 'rows', axis=0, tiled=True)  77.5 us
    all_to_all x1, blocking collectives, on_device(): lax.all_to_all(rounded, 'dirs', split_axis=2, concat_axis=0, tiled=True)  39.4 us
    all_to_all x1, waiting for transfers between devices, on_device(): lax.all_to_all(gained, 'dirs', split_axis=0, concat_axis=2, tiled=True)  35.9 us
    dynamic_slice x8, local copies, waits for them, and re-layouts, on_device(): lax.scan(row_step, (start_gain, start_value), (jnp.moveaxis(couple, 1, 0)...  29 us
    dynamic_update_slice x32, other arithmetic, on_device(): lax.scan(device_step, (jnp.ones_like(block_gain), jnp.zeros_like(block_st...  25.5 us
    all_gather x1, blocking collectives, on_device(): lax.all_gather(block_gain[None], 'rows', axis=0, tiled=True)  25.4 us
    add x16, other arithmetic, compose(): following_part[0] * preceding_part[1] + following_part[1]  23.1 us
  transfers between devices with their start and end apart: 2, of which 2 were waited for; matrix products, arithmetic and copies ran while one was open for 0% of the time, Pallas kernels for 0%

commit v1 on v0

v1 whole, which is shorter than its diff:
```python
import functools

import jax
import jax.numpy as jnp
from jax import lax
from jax.experimental import pallas as pl
from jax.experimental.pallas import tpu as pltpu
from jax.sharding import PartitionSpec as P

SHIFT = 2
GROUP = 8
f32 = jnp.float32
bf16 = jnp.bfloat16
MESH = pl.DeviceIdType.MESH
VMEM_BYTES = 48 * 1024 * 1024


def cost(microseconds):
    return pl.CostEstimate(
        flops=0, bytes_accessed=int(microseconds * 3_000_000), transcendentals=0
    )


def weights(coupling, sea):
    return coupling * sea, sea * (1.0 - coupling)


def visit_order(shape, backward):
    row = lax.broadcasted_iota(jnp.int32, shape, 0)
    return shape[0] - 1 - row if backward else row


def rolled(x, steps, backward):
    rows = x.shape[0]
    return pltpu.roll(x, (rows - steps if backward else steps) % rows, 0)


def compose_kernel(quadrant, previous, coupling, sea, gain, state):
    d = pl.program_id(0)
    bands = previous.shape[1]

    def run(backward):
        couple, weight = weights(coupling[0], sea[...])
        rows = couple.shape[0]
        order = visit_order(couple.shape, backward)
        after = jnp.where(order < rows - 1, rolled(couple, rows - 1, backward), 1.0)
        span = 1
        while span < rows - 1:
            after = after * jnp.where(order < rows - span, rolled(after, rows - span, backward), 1.0)
            span *= 2
        gain[0] = jnp.sum(jnp.where(order == 0, couple * after, 0.0), axis=0, keepdims=True)
        total = weight * after

        def group(q, _):
            values = previous[0, pl.ds(q * GROUP, GROUP)].astype(f32)
            state[q, 0] = jnp.sum(values * total[None], axis=1)
            return 0

        lax.fori_loop(0, bands // GROUP, group, 0)

    pl.when(quadrant[d] % 2 == 0)(lambda: run(False))
    pl.when(quadrant[d] % 2 == 1)(lambda: run(True))


def compose_rows(quadrant, previous, coupling, sea):
    dirs, bands, rows, columns = previous.shape
    groups = bands // GROUP
    return pl.pallas_call(
        compose_kernel,
        grid=(dirs,),
        in_specs=[
            pl.BlockSpec(memory_space=pltpu.SMEM),
            pl.BlockSpec((1, bands, rows, columns), lambda d: (d, 0, 0, 0)),
            pl.BlockSpec((1, rows, columns), lambda d: (d, 0, 0)),
            pl.BlockSpec((rows, columns), lambda d: (0, 0)),
        ],
        out_specs=[
            pl.BlockSpec((1, 1, columns), lambda d: (d, 0, 0)),
            pl.BlockSpec((groups, 1, GROUP, columns), lambda d: (0, d, 0, 0)),
        ],
        out_shape=[
            jax.ShapeDtypeStruct((dirs, 1, columns), f32),
            jax.ShapeDtypeStruct((groups, dirs, GROUP, columns), f32),
        ],
        cost_estimate=cost(5),
        name="compose_rows",
    )(quadrant, previous, coupling, sea)


HALO_ARRAYS = 4


def scan_kernel(
    count, dir_count, chunks, gain, state, boundary, backward, *refs
):
    shared, refs = refs[:HALO_ARRAYS], refs[HALO_ARRAYS:]
    out, refs = refs[0], refs[1:]
    halos, refs = (refs[:HALO_ARRAYS], refs[HALO_ARRAYS : 2 * HALO_ARRAYS]), refs[2 * HALO_ARRAYS :]
    (
    gains, got_core, half_total, got_pair, plane, chain_in, chain_out, pair_in, pair_out, core_out,
    gain_send, gain_recv, core_send, core_recv, pair_send, pair_recv,
    chain_send, chain_recv, back_send, back_recv, last_send, last_recv, halo_send, halo_recv,
    ) = refs
    me = lax.axis_index("rows")
    c, x, z = me % 2, (me // 2) % 2, me // 4
    depth = count // 4
    core_peer = me + 1 - 2 * c
    pair_peer = me + 2 - 4 * x
    cross_peer = core_peer + 2 - 4 * x
    dirs = gain.shape[0]
    size = dirs // chunks
    peers = (core_peer, pair_peer, cross_peer)

    def part(j):
        return pl.ds(j * size, size)

    barrier = pltpu.get_barrier_semaphore()
    for peer in peers:
        pl.semaphore_signal(barrier, inc=1, device_id={"rows": peer}, device_id_type=MESH)

    @pl.when(z > 0)
    def _():
        pl.semaphore_signal(barrier, inc=1, device_id={"rows": me - 4}, device_id_type=MESH)

    @pl.when(z < depth - 1)
    def _():
        pl.semaphore_signal(barrier, inc=1, device_id={"rows": me + 4}, device_id_type=MESH)

    mine = lax.axis_index("dirs")
    higher, lower = (mine + 1) % dir_count, (mine + dir_count - 1) % dir_count
    neighbours = (higher, lower) if dir_count > 2 else (higher,)
    for peer in neighbours:
        pl.semaphore_signal(barrier, inc=1, device_id={"dirs": peer}, device_id_type=MESH)
    pl.semaphore_wait(
        barrier, 3 + len(neighbours) + (z > 0).astype(jnp.int32) + (z < depth - 1).astype(jnp.int32)
    )

    def remote(src, dst, send, recv, peer):
        return pltpu.make_async_remote_copy(
            src_ref=src, dst_ref=dst, send_sem=send, recv_sem=recv,
            device_id={"rows": peer}, device_id_type=MESH,
        )

    gain_copies = [
        remote(gain, gains.at[i], gain_send.at[i], gain_recv.at[i], peer) for i, peer in enumerate(peers)
    ]
    core_copies = [
        remote(state.at[1 - c, :, part(j)], got_core.at[:, part(j)], core_send.at[j], core_recv.at[j], core_peer)
        for j in range(chunks)
    ]
    pair_copies = [
        remote(half_total.at[1 - x, part(j)], got_pair.at[part(j)], pair_send.at[j], pair_recv.at[j], pair_peer)
        for j in range(chunks)
    ]
    back_copies = [
        remote(pair_out.at[part(j)], pair_in.at[x, part(j)], back_send.at[j], back_recv.at[j], pair_peer)
        for j in range(chunks)
    ]
    last_copies = [
        remote(core_out.at[:, part(j)], out.at[c, :, part(j)], last_send.at[j], last_recv.at[j], core_peer)
        for j in range(chunks)
    ]

    for copy in gain_copies:
        copy.start()
    for copy in core_copies:
        copy.start()
    halo_copies = []
    for way, (peer, start) in enumerate(((lower, 0), (higher, dirs - SHIFT))):
        for i, array in enumerate(shared):
            halo_copies.append(
                pltpu.make_async_remote_copy(
                    src_ref=array.at[pl.ds(start, SHIFT)], dst_ref=halos[way][i],
                    send_sem=halo_send.at[way, i], recv_sem=halo_recv.at[way, i],
                    device_id={"dirs": peer}, device_id_type=MESH,
                )
            )
            halo_copies[-1].start()

    back = backward[...]
    c_bit, x_bit = c.astype(f32), x.astype(f32)
    core_after = c_bit + back - 2.0 * c_bit * back
    pair_after = x_bit + back - 2.0 * x_bit * back
    for copy in gain_copies:
        copy.wait_recv()
    core_mine, core_theirs = gain[...], gains[0]
    pair_mine, pair_theirs = core_mine * core_theirs, gains[1] * gains[2]
    plane_gain = pair_mine * pair_theirs

    def total(after, mine, theirs):
        return after * mine + (1.0 - after), (1.0 - after) * theirs + after

    core_a, core_b = total(core_after, core_mine, core_theirs)
    pair_a, pair_b = total(pair_after, pair_mine, pair_theirs)

    def cut(v, j):
        return v[j * size : (j + 1) * size]

    for j in range(chunks):
        core_copies[j].wait_recv()
        half_total[:, part(j)] = (
            cut(core_a, j)[None] * got_core[:, part(j)] + cut(core_b, j)[None] * state[c, :, part(j)]
        )
        pair_copies[j].start()
    for j in range(chunks):
        pair_copies[j].wait_recv()
        plane[part(j)] = cut(pair_a, j) * got_pair[part(j)] + cut(pair_b, j) * half_total[x, part(j)]

    upper = (2 * z >= depth).astype(jnp.int32)
    mine_at = 2 * c + x

    def chain(j, way):
        step = 1 - 2 * way
        has_before = jnp.where(way == 0, z > 0, z < depth - 1)
        has_after = jnp.where(way == 0, z < depth - 1, z > 0)
        copy = remote(
            chain_out.at[way, part(j)], chain_in.at[way, part(j)],
            chain_send.at[way, j], chain_recv.at[way, j], me + 4 * step,
        )

        @pl.when(has_before)
        def _():
            copy.wait_recv()

        @pl.when(jnp.logical_not(has_before))
        def _():
            chain_in[way, part(j)] = boundary[part(j), mine_at]

        @pl.when(has_after)
        def _():
            chain_out[way, part(j)] = cut(plane_gain, j) * chain_in[way, part(j)] + plane[part(j)]
            copy.start()

    def split(after, mine, theirs):
        return after * theirs + (1.0 - after), (1.0 - after) * mine + after

    pair_p, pair_q = split(pair_after, pair_mine, pair_theirs)
    core_p, core_q = split(core_after, core_mine, core_theirs)
    for j in range(chunks):
        chain(j, upper)
        chain(j, 1 - upper)
        entering = jnp.where(cut(back, j) > 0.5, chain_in[1, part(j)], chain_in[0, part(j)])
        pair_out[part(j)] = cut(pair_q, j) * entering + (1.0 - cut(pair_after, j)) * half_total[x, part(j)]
        back_copies[j].start()
        pair_in[x, part(j)] = cut(pair_p, j) * entering + cut(pair_after, j) * got_pair[part(j)]
    for j in range(chunks):
        back_copies[j].wait_recv()
        entering = pair_in[:, part(j)]
        core_out[:, part(j)] = (
            cut(core_q, j)[None] * entering + (1.0 - cut(core_after, j))[None] * state[c, :, part(j)]
        )
        last_copies[j].start()
        out[c, :, part(j)] = cut(core_p, j)[None] * entering + cut(core_after, j)[None] * got_core[:, part(j)]
    for j in range(chunks):
        last_copies[j].wait_recv()
    for copy in halo_copies:
        copy.wait_recv()
    for copy in halo_copies + gain_copies + core_copies + pair_copies + back_copies + last_copies:
        copy.wait_send()

    def drain(j, way):
        copy = remote(
            chain_out.at[way, part(j)], chain_in.at[way, part(j)],
            chain_send.at[way, j], chain_recv.at[way, j], me + 4 * (1 - 2 * way),
        )

        @pl.when(z < depth - 1 if way == 0 else z > 0)
        def _():
            copy.wait_send()

    for j in range(chunks):
        drain(j, 0)
        drain(j, 1)


def scan_devices(count, dir_count, gain, state, boundary, backward, shared):
    groups, dirs, _, columns = state.shape
    chunks = 3 if dirs % 3 == 0 else 1
    quarter = groups // 4 * GROUP
    state = state.reshape(2, 2, dirs, quarter, columns)
    boundary = boundary.reshape(dirs, 4, quarter, columns)
    vmem = pl.BlockSpec(memory_space=pltpu.VMEM)
    part = (dirs, quarter, columns)
    dma = pltpu.SemaphoreType.DMA
    anywhere = pl.BlockSpec(memory_space=pl.ANY)
    halos = [jax.ShapeDtypeStruct((SHIFT,) + a.shape[1:], a.dtype) for a in shared] * 2
    out, *halos = pl.pallas_call(
        functools.partial(scan_kernel, count, dir_count, chunks),
        in_specs=[vmem] * 4 + [anywhere] * HALO_ARRAYS,
        out_specs=[vmem] + [anywhere] * (2 * HALO_ARRAYS),
        out_shape=[jax.ShapeDtypeStruct(state.shape, f32)] + halos,
        scratch_shapes=[
            pltpu.VMEM((3, dirs, 1, columns), f32),
            pltpu.VMEM((2,) + part, f32),
            pltpu.VMEM((2,) + part, f32),
            pltpu.VMEM(part, f32),
            pltpu.VMEM(part, f32),
            pltpu.VMEM((2,) + part, f32),
            pltpu.VMEM((2,) + part, f32),
            pltpu.VMEM((2,) + part, f32),
            pltpu.VMEM(part, f32),
            pltpu.VMEM((2,) + part, f32),
            dma((3,)), dma((3,)),
            dma((chunks,)), dma((chunks,)),
            dma((chunks,)), dma((chunks,)),
            dma((2, chunks)), dma((2, chunks)),
            dma((chunks,)), dma((chunks,)),
            dma((chunks,)), dma((chunks,)),
            dma((2, HALO_ARRAYS)), dma((2, HALO_ARRAYS)),
        ],
        compiler_params=pltpu.CompilerParams(
            collective_id=0, has_side_effects=True, vmem_limit_bytes=VMEM_BYTES
        ),
        cost_estimate=cost(35),
        name="scan_devices",
    )(gain, state, boundary, backward, *shared)
    return out.reshape(groups, dirs, GROUP, columns), halos[:HALO_ARRAYS], halos[HALO_ARRAYS:]


def settle_kernel(quadrant, previous, coupling, sea, entering, matrix, carry, *rest):
    swept = rest[-1]
    outs = rest[:-1]
    d = pl.program_id(0)
    _, bands, rows, columns = previous.shape
    block = carry.shape[-1]
    pieces = columns // block

    def sweep(backward):
        couple, weight = weights(coupling[0], sea[...])
        order = visit_order(couple.shape, backward)
        first = jnp.where(order == 0, couple, 0.0)
        spans, reach, span = [], couple, 1
        while span < rows:
            spans.append((span, jnp.where(order >= span, reach, 0.0)))
            reach = jnp.where(order >= span, reach * rolled(reach, span, backward), reach)
            span *= 2

        def group(q, _):
            inflow = entering[q, 0]
            for r in range(GROUP):
                value = weight * previous[0, q * GROUP + r].astype(f32) + first * inflow[r : r + 1]
                for span, factor in spans:
                    value = value + factor * rolled(value, span, backward)
                swept[q * GROUP + r] = value
            return 0

        lax.fori_loop(0, bands // GROUP, group, 0)

    pl.when(quadrant[d] % 2 == 0)(lambda: sweep(False))
    pl.when(quadrant[d] % 2 == 1)(lambda: sweep(True))

    def columns_solve(sideways):
        upper = matrix[0]
        whole = jnp.concatenate(
            [upper, jnp.concatenate([upper[:, :block], jnp.zeros((block, block), bf16)], axis=1)], axis=0
        )
        before = None
        for k in range(pieces - 1, -1, -1) if sideways else range(pieces):
            here = slice(k * block, (k + 1) * block)
            x = swept[:, :, here].reshape(bands * rows, block)
            high = x.astype(bf16)
            low = (x - high.astype(f32)).astype(bf16)
            both = jnp.dot(
                jnp.concatenate([high, low], axis=1), whole, preferred_element_type=f32
            )
            y = both[:, :block] + both[:, block:]
            if before is not None:
                last = before[:, :1] if sideways else before[:, block - 1 :]
                y = y + last * carry[0]
            before = y
            masked = y.reshape(bands, rows, block) * sea[:, here][None]
            outs[0][0, :, :, here] = masked.astype(bf16)
            if len(outs) > 1:
                outs[1][0, :, :, here] = masked

    pl.when(quadrant[d] // 2 == 0)(lambda: columns_solve(False))
    pl.when(quadrant[d] // 2 == 1)(lambda: columns_solve(True))


def settle(quadrant, previous, coupling, sea, entering, matrix, carry, keep):
    dirs, bands, rows, columns = previous.shape
    block = carry.shape[-1]
    field = pl.BlockSpec((1, bands, rows, columns), lambda d: (d, 0, 0, 0))
    kinds = [bf16, f32] if keep else [bf16]
    return pl.pallas_call(
        settle_kernel,
        grid=(dirs,),
        in_specs=[
            pl.BlockSpec(memory_space=pltpu.SMEM),
            field,
            pl.BlockSpec((1, rows, columns), lambda d: (d, 0, 0)),
            pl.BlockSpec((rows, columns), lambda d: (0, 0)),
            pl.BlockSpec((bands // GROUP, 1, GROUP, columns), lambda d: (0, d, 0, 0)),
            pl.BlockSpec((1, block, 2 * block), lambda d: (d, 0, 0)),
            pl.BlockSpec((1, 1, block), lambda d: (d, 0, 0)),
        ],
        out_specs=[field] * len(kinds),
        out_shape=[jax.ShapeDtypeStruct(previous.shape, kind) for kind in kinds],
        scratch_shapes=[pltpu.VMEM((bands, rows, columns), f32)],
        compiler_params=pltpu.CompilerParams(vmem_limit_bytes=VMEM_BYTES),
        cost_estimate=cost(dirs),
        name="settle_keep" if keep else "settle_halo",
    )(quadrant, previous, coupling, sea, entering, matrix, carry)


def source_kernel(dirs, coef, wet, settled, center, above, below, above_halo, below_halo, out):
    d = pl.program_id(0)
    bands = center.shape[1]

    def run(above, below):
        wet_cells = wet[...]

        def one(f, onward, against):
            energy = center[0, f].astype(f32)
            onward, against = onward.astype(f32), against.astype(f32)
            source = coef[f] * (
                energy * energy * (onward + against) - 2.0 * energy * onward * against
            )
            out[0, f] = (settled[0, f] + wet_cells * source.astype(bf16).astype(f32)).astype(bf16)

        nothing = jnp.zeros(wet.shape, f32)
        one(0, above[0, 1], nothing)
        one(bands - 1, nothing, below[0, bands - 2])

        def body(f, _):
            one(f, above[0, f + 1], below[0, f - 1])
            return 0

        lax.fori_loop(1, bands - 1, body, 0, unroll=6 if (bands - 2) % 6 == 0 else 1)

    top, low = d + SHIFT >= dirs, d < SHIFT
    for top_here in (False, True):
        for low_here in (False, True):
            pl.when((top == top_here) & (low == low_here))(
                functools.partial(
                    run, above_halo if top_here else above, below_halo if low_here else below
                )
            )


def add_source(coef, wet, settled, rounded, above_halo, below_halo):
    dirs, bands, rows, columns = rounded.shape
    shape = (1, bands, rows, columns)

    def at(place):
        return pl.BlockSpec(shape, lambda d: (place(d), 0, 0, 0))

    return pl.pallas_call(
        functools.partial(source_kernel, dirs),
        grid=(dirs,),
        in_specs=[
            pl.BlockSpec(memory_space=pltpu.SMEM),
            pl.BlockSpec((rows, columns), lambda d: (0, 0)),
            at(lambda d: d),
            at(lambda d: d),
            at(lambda d: jnp.minimum(d + SHIFT, dirs - 1)),
            at(lambda d: jnp.maximum(d - SHIFT, 0)),
            at(lambda d: jnp.maximum(d + SHIFT - dirs, 0)),
            at(lambda d: jnp.minimum(d, SHIFT - 1)),
        ],
        out_specs=at(lambda d: d),
        out_shape=jax.ShapeDtypeStruct(rounded.shape, bf16),
        compiler_params=pltpu.CompilerParams(vmem_limit_bytes=VMEM_BYTES),
        cost_estimate=cost(10),
        name="add_source",
    )(coef, wet, settled, rounded, rounded, rounded, above_halo, below_halo)


def on_device(
    row_devices, dir_devices,
    previous, boundary, row_coupling, cross_gain, block_inverse, quadrant, sea_mask, wet_tiles, quad_coef,
):
    dirs, bands, rows, columns = previous.shape
    block = block_inverse.shape[-1]
    sea = sea_mask.astype(f32)
    wet = jnp.repeat(wet_tiles.astype(f32), block, axis=1)
    up = [(i, (i + 1) % dir_devices) for i in range(dir_devices)]
    down = [(i, (i - 1) % dir_devices) for i in range(dir_devices)]

    def from_above(a):
        return lax.ppermute(a, "dirs", down)

    def from_below(a):
        return lax.ppermute(a, "dirs", up)

    sideways = quadrant // 2 == 1
    matrix = jnp.where(
        sideways[:, None, None], block_inverse, jnp.swapaxes(block_inverse, 1, 2)
    )
    carry = cross_gain[:, None] * jnp.where(
        sideways[:, None], block_inverse[:, block - 1], block_inverse[:, :, 0]
    )
    high = lax.reduce_precision(matrix, 8, 7)
    low = (matrix - high).astype(bf16)
    high = high.astype(bf16)
    paired = jnp.concatenate([high, low], 2)
    marked = jnp.concatenate(
        [carry, jnp.broadcast_to(quadrant.astype(f32)[:, None], carry.shape)], 1
    )[:, None, :]
    carry = carry[:, None, :]

    gain, state = compose_rows(quadrant, previous, row_coupling, sea)
    backward = jnp.broadcast_to((quadrant % 2).astype(f32)[:, None, None], (dirs, 1, columns))
    entering, above, below = scan_devices(
        row_devices, dir_devices, gain, state, boundary, backward,
        (previous, row_coupling, paired, marked),
    )
    enter_above = from_above(entering[:, :SHIFT])
    enter_below = from_below(entering[:, dirs - SHIFT :])

    rounded, settled = settle(
        quadrant, previous, row_coupling, sea, entering, paired, carry, True
    )

    def halo(parts, inflow):
        prior, coupling, half, marks = parts
        quad = marks[:, 0, block].astype(jnp.int32)
        return settle(quad, prior, coupling, sea, inflow, half, marks[:, :, :block], False)[0]

    above_halo = halo(above, enter_above)
    below_halo = halo(below, enter_below)
    return add_source(quad_coef, wet, settled, rounded, above_halo, below_halo)


def solution(mesh):
    in_specs = (
        P("dirs", None, "rows", None),
        P("dirs", None, None),
        P("dirs", "rows", None),
        P("dirs"),
        P("dirs", None, None),
        P("dirs"),
        P("rows", None),
        P("rows", None),
        P(),
    )
    out_specs = P("dirs", None, "rows", None)
    return jax.shard_map(
        functools.partial(on_device, mesh.shape["rows"], mesh.shape["dirs"]),
        mesh=mesh, in_specs=in_specs, out_specs=out_specs, check_vma=False,
    )
```

time: 641 us -> 97.4 us (0.15); the launches traced: 633 us -> 96.3 us
  local copies, waits for them, and re-layouts: 268 us -> 3.56 us
  other arithmetic: 159 us -> 5.45 us
  waiting for transfers between devices: 113 us -> 0.01 us
  Pallas kernels: 0 us -> 85 us
  blocking collectives: 64.8 us -> 0 us
  between operations: 13.6 us -> 0.19 us
  matrix products: 8.55 us -> 0 us
    dynamic_update_slice x24 -> x0, local copies, waits for them, and re-layouts: 141 us -> none  [on_device(): lax.scan(row_step, (start_gain, start_value), (jnp.moveaxis(couple, 1, 0)...]
    pallas_call x0 -> x6, Pallas kernels: none -> 85 us  [the longest x1 48.8 us: scan_devices(): pl.pallas_call(functools.partial(scan_kernel, count, dir_count, chunks),...]
    all_gather x1 -> x0, waiting for transfers between devices: 77.5 us -> none  [on_device(): lax.all_gather(block_state[None], 'rows', axis=0, tiled=True)]
    add x27 -> x0, other arithmetic: 48.9 us -> none  [the longest x16 23.1 us: compose(): following_part[0] * preceding_part[1] + following_part[1]]
    rev x5 -> x0, local copies, waits for them, and re-layouts: 47.5 us -> none  [the longest x1 12.5 us: on_device(): jnp.flip(settled, 3)]
    all_to_all x1 -> x0, blocking collectives: 39.4 us -> none  [on_device(): lax.all_to_all(rounded, 'dirs', split_axis=2, concat_axis=0, tiled=True)]
    all_to_all x1 -> x0, waiting for transfers between devices: 35.9 us -> none  [on_device(): lax.all_to_all(gained, 'dirs', split_axis=0, concat_axis=2, tiled=True)]
    dynamic_slice x9 -> x0, local copies, waits for them, and re-layouts: 29.7 us -> none  [the longest x8 29 us: on_device(): lax.scan(row_step, (start_gain, start_value), (jnp.moveaxis(couple, 1, 0)...]
  transfers between devices with their start and end apart: 2 -> 2, of which waited for: 2 -> 0; matrix products, arithmetic and copies ran while one was open for 0% -> 0% of each run, Pallas kernels for 0% -> 16%
where the time goes in v1:
time: 97.4 us; the launch traced here: 96.3 us
  Pallas kernels  85 us (87%)
  other arithmetic  5.45 us (6%)
  local copies, waits for them, and re-layouts  3.56 us (4%)
  starting transfers between devices  2.09 us (2%)
    pallas_call x1, Pallas kernels, scan_devices(): pl.pallas_call(functools.partial(scan_kernel, count, dir_count, chunks),...  48.8 us
    pallas_call x3, Pallas kernels, settle(): pl.pallas_call(settle_kernel, grid=(dirs,), in_specs=[pl.BlockSpec(memory...  17.2 us
    pallas_call x1, Pallas kernels, add_source(): pl.pallas_call(functools.partial(source_kernel, dirs), grid=(dirs,), in_s...  10.4 us
    pallas_call x1, Pallas kernels, compose_rows(): pl.pallas_call(compose_kernel, grid=(dirs,), in_specs=[pl.BlockSpec(memor...  8.61 us
    unnamed x19, local copies, waits for them, and re-layouts  3.29 us
  transfers between devices with their start and end apart: 2, of which 0 were waited for; matrix products, arithmetic and copies ran while one was open for 0% of the time, Pallas kernels for 16%

profile of v1, /device:TPU:0, one launch (start us, length us, event | category | flops | bytes accessed | tf_op | source)
XLA Modules:
  0.0 96.3 jit_solution(5243984969700846116)
XLA Ops:
  0.0 0.7 fusion.5
  0.7 0.7 fusion.7
  1.4 1.3 %convert_element_type.29.sea = f32[8,512]{1,0:T(8,128)} convert(s32[8,512]{1,0:T(8,128)} %param.15) | non-fusion elementwise | flops 4096 | bytes 32768 | tf_op jit(solution)/shard_map/convert_element_type | solution.py:475
  2.7 1.4 %copy.15 = f32[12,128,128]{1,2,0:T(8,128)S(1)} copy(f32[12,128,128]{2,1,0:T(8,128)} %param.13) | data formatting | bytes 1572864 | tf_op args[4]
  4.2 0.0 copy-start
  4.2 1.5 %reduce-precision_convert_fusion = (bf16[12,128,128]{2,1,0:T(8,128)(2,1)S(1)}, bf16[12,128,128]{2,1,0:T(8,128)(2,1)S(1)}) fusion(f32[12,128,128]{2,1,0:T(8,128)} %param.13, f32[12,128,128]{1,2,0:T(8,128)S(1)} %copy.15, pred[12]{0:T(512)(128)(4,1)S(1)} %fusion.5), kind=kLoop, calls=%fused_computation.1 | loop fusion | flops 983040 | bytes 2359308 | tf_op jit(solution)/shard_map/convert_element_type | solution.py:495
  5.7 0.9 fusion.3
  6.6 0.1 fusion.2
  6.7 0.1 broadcast_in_dim.44
  6.8 0.1 pad_maximum_fusion.refs_2_.matrix
  6.9 8.6 %compose_rows.1 = (f32[12,1,512]{2,1,0:T(1,128)}, f32[4,12,8,512]{3,2,1,0:T(8,128)}) custom-call(s32[12]{0:T(128)} %quadrant.3, bf16[12,32,8,512]{3,2,1,0:T(8,128)(2,1)} %previous.3, f32[12,8,512]{2,1,0:T(8,128)} %coupling.3, f32[8,512]{1,0:T(8,128)} %convert_element_type.29.sea), custom_call_target="tpu_custom_call" | custom-call | bytes 15000000 | tf_op jit(solution)/shard_map/compose_rows/pallas_call | solution.py:68
  15.5 0.1 broadcast_in_dim.41.backward
  15.6 0.0 copy-start.2
  15.6 1.1 %copy-done.2 = f32[4,12,8,512]{3,2,1,0:T(8,128)S(1)} copy-done((f32[4,12,8,512]{3,2,1,0:T(8,128)S(1)}, f32[4,12,8,512]{3,2,1,0:T(8,128)}, u32[]{:S(2)}) %copy-start.2) | copy-done | bytes 786456
  16.7 0.7 copy-done.4
  17.5 48.8 %scan_devices.1 = (f32[2,2,12,8,512]{4,3,2,1,0:T(8,128)S(1)}, bf16[2,32,8,512]{3,2,1,0:T(8,128)(2,1)S(1)}, f32[2,8,512]{2,1,0:T(8,128)S(1)}, bf16[2,128,256]{2,1...) custom-call(f32[12,1,512]{2,1,0:T(1,128)S(1)} %copy-done.4, ...), custom_call_target="tpu_custom_call" | custom-call | bytes 105000000 | tf_op jit(solution)/shard_map/scan_devices/pallas_call | solution.py:287
  66.3 0.6 collective-permute-start.1
  66.9 1.5 %collective-permute-start = (f32[4,2,8,512]{3,2,1,0:T(8,128)S(1)}, f32[4,2,8,512]{3,2,1,0:T(8,128)S(1)}, u32[]{:S(2)}, u32[]{:S(2)}) collective-permute-start(f32[4,2,8,512]{3,2,1,0:T(8,128)S(1)} %get-tuple-element.34), channel_id=1, source_target_pairs={{0,1},{1,0},{2,3},{3,2},{4,5},{5,4},{6,7},{7,6},{8,9},{9,8},{10,11... | collective-permute-start | bytes 393224 | tf_op jit(solution)/shard_map/ppermute | solution.py:481
  68.4 0.1 broadcast_bitcast_fusion.wet
  68.5 13.0 %settle_keep.1 = (bf16[12,32,8,512]{3,2,1,0:T(8,128)(2,1)S(1)}, f32[12,32,8,512]{3,2,1,0:T(8,128)}) custom-call(s32[12]{0:T(128)S(1)} %copy-done.5, bf16[12,32,8,512]{3,2,1,0:T(8,128)(2,1)} %previous.3, f32[12,8,512]{2,1,0:T(8,128)S(1)} %copy-done, f32[8,512]{1,0:T(8,128)S(1)} %copy-done.3, f32[4,12,8,512]{3,2,1,0:T(8,128)S(1)} %bitcast.26, ...), custom_call_target="tpu_custom_call" | custom-call | bytes 36000000 | tf_op jit(solution)/shard_map/settle_keep/pallas_call | solution.py:385
  81.5 0.2 convert_reduce_fusion
  81.7 2.1 %settle_halo.3.below_halo = bf16[2,32,8,512]{3,2,1,0:T(8,128)(2,1)S(1)} custom-call(s32[2]{0:T(128)S(1)} %get-tuple-element.39.quadrant, bf16[2,32,8,512]{3,2,1,0:T(8,128)(2,1)S(1)} %get-tuple-element.28.previous, f32[2,8,512]{2,1,0:T(8,128)S(1)} %get-tuple-element.29.coupling, f32[8,512]{1,0:T(8,128)S(1)} %copy-done.3, ...), custom_call_target="tpu_custom_call" | custom-call | bytes 6000000 | tf_op jit(solution)/shard_map/settle_halo/pallas_call | solution.py:385
  83.8 2.1 %settle_halo.2.above_halo = bf16[2,32,8,512]{3,2,1,0:T(8,128)(2,1)S(1)} custom-call(s32[2]{0:T(128)S(1)} %get-tuple-element.40.quadrant, bf16[2,32,8,512]{3,2,1,0:T(8,128)(2,1)S(1)} %get-tuple-element.24.previous, f32[2,8,512]{2,1,0:T(8,128)S(1)} %get-tuple-element.25.coupling, f32[8,512]{1,0:T(8,128)S(1)} %copy-done.3, ...), custom_call_target="tpu_custom_call" | custom-call | bytes 6000000 | tf_op jit(solution)/shard_map/settle_halo/pallas_call | solution.py:385
  86.0 10.4 %add_source.1 = bf16[12,32,8,512]{3,2,1,0:T(8,128)(2,1)} custom-call(f32[32]{0:T(128)S(1)} %copy-done.6, f32[8,512]{1,0:T(8,128)S(1)} %broadcast_bitcast_fusion.wet, f32[12,32,8,512]{3,2,1,0:T(8,128)} %get-tuple-element.21.settled, bf16[12,32,8,512]{3,2,1,0:T(8,128)(2,1)S(1)} %get-tuple-element.22.center.above.below, ...), custom_call_target="tpu_custom_call" | custom-call | bytes 30000000 | tf_op jit(solution)/shard_map/add_source/pallas_call | solution.py:448
  (23 shorter events, 0.1 us)
Async XLA Ops:
  0.0 5.7 %copy-start.7 = (f32[12]{0:T(128)S(1)}, f32[12]{0:T(128)}, u32[]{:S(2)}) copy-start(f32[12]{0:T(128)} %param.12) | copy-start | bytes 148
  4.2 11.4 %copy-start = (f32[12,8,512]{2,1,0:T(8,128)S(1)}, f32[12,8,512]{2,1,0:T(8,128)}, u32[]{:S(2)}) copy-start(f32[12,8,512]{2,1,0:T(8,128)} %coupling.3) | copy-start | bytes 589828
  4.2 11.4 %copy-start.1 = (f32[12,32,512]{2,1,0:T(8,128)S(1)}, f32[12,32,512]{2,1,0:T(8,128)}, u32[]{:S(2)}) copy-start(f32[12,32,512]{2,1,0:T(8,128)} %param.10) | copy-start | bytes 2359300
  15.6 1.1 %copy-start.2 = (f32[4,12,8,512]{3,2,1,0:T(8,128)S(1)}, f32[4,12,8,512]{3,2,1,0:T(8,128)}, u32[]{:S(2)}) copy-start(f32[4,12,8,512]{3,2,1,0:T(8,128)} %get-tuple-element.19) | copy-start | bytes 2359300
  16.7 0.7 copy-start.4
  17.5 50.9 %copy-start.8 = (s32[8,4]{0,1:T(4,128)S(1)}, s32[8,4]{0,1:T(4,128)}, u32[]{:S(2)}) copy-start(s32[8,4]{0,1:T(4,128)} %param.16) | copy-start | bytes 388
  17.5 51.0 %copy-start.3 = (f32[8,512]{1,0:T(8,128)S(1)}, f32[8,512]{1,0:T(8,128)}, u32[]{:S(2)}) copy-start(f32[8,512]{1,0:T(8,128)} %convert_element_type.29.sea) | copy-start | bytes 49156
  17.5 51.0 %copy-start.5 = (s32[12]{0:T(128)S(1)}, s32[12]{0:T(128)}, u32[]{:S(2)}) copy-start(s32[12]{0:T(128)} %quadrant.3) | copy-start | bytes 148
  66.3 15.4 %collective-permute-start.1 = (f32[4,2,8,512]{3,2,1,0:T(8,128)S(1)}, f32[4,2,8,512]{3,2,1,0:T(8,128)S(1)}, u32[]{:S(2)}, u32[]{:S(2)}) collective-permute-start(f32[4,2,8,512]{3,2,1,0:T(8,128)S(1)} %get-tuple-element.33), channel_id=1, source_target_pairs={{0,1},{1,0},{2,3},{3,2},{4,5},{5,4},{6,7},{7,6},{8,9},{9,8},{10,11... | collective-permute-start | bytes 393224 | tf_op jit(solution)/shard_map/ppermute | solution.py:484
  66.9 16.9 %collective-permute-start = (f32[4,2,8,512]{3,2,1,0:T(8,128)S(1)}, f32[4,2,8,512]{3,2,1,0:T(8,128)S(1)}, u32[]{:S(2)}, u32[]{:S(2)}) collective-permute-start(f32[4,2,8,512]{3,2,1,0:T(8,128)S(1)} %get-tuple-element.34), channel_id=1, source_target_pairs={{0,1},{1,0},{2,3},{3,2},{4,5},{5,4},{6,7},{7,6},{8,9},{9,8},{10,11... | collective-permute-start | bytes 393224 | tf_op jit(solution)/shard_map/ppermute | solution.py:481
  68.5 17.5 %copy-start.6 = (f32[32]{0:T(128)S(1)}, f32[32]{0:T(128)}, u32[]{:S(2)}) copy-start(f32[32]{0:T(128)} %coef.1) | copy-start | bytes 388

commit v2 on v1

v2 whole, which is shorter than its diff:
```python
import functools

import jax
import jax.numpy as jnp
from jax import lax
from jax.experimental import pallas as pl
from jax.experimental.pallas import tpu as pltpu
from jax.sharding import PartitionSpec as P

SHIFT = 2
f32 = jnp.float32
bf16 = jnp.bfloat16
MESH = pl.DeviceIdType.MESH
VMEM_BYTES = 48 * 1024 * 1024


def cost(microseconds):
    return pl.CostEstimate(
        flops=0, bytes_accessed=int(microseconds * 3_000_000), transcendentals=0
    )


def weights(coupling, sea):
    return coupling * sea, sea * (1.0 - coupling)


def visit_order(shape, backward):
    row = lax.broadcasted_iota(jnp.int32, shape, 0)
    return shape[0] - 1 - row if backward else row


def rolled(x, steps, backward):
    rows = x.shape[0]
    return pltpu.roll(x, (rows - steps if backward else steps) % rows, 0)


def row_weights(coupling, sea, backward):
    couple, weight = weights(coupling, sea)
    rows = couple.shape[0]
    order = visit_order(couple.shape, backward)
    after = jnp.where(order < rows - 1, rolled(couple, rows - 1, backward), 1.0)
    span = 1
    while span < rows - 1:
        after = after * jnp.where(order < rows - span, rolled(after, rows - span, backward), 1.0)
        span *= 2
    gain = jnp.sum(jnp.where(order == 0, couple * after, 0.0), axis=0, keepdims=True)
    return weight * after, gain


HALO_ARRAYS = 4


def scan_kernel(
    count, dir_count, chunks, boundary, sea_mask, previous, coupling, inverse, marks, out, *refs
):
    shared = (previous, coupling, inverse, marks)
    halos, refs = refs[:HALO_ARRAYS], refs[HALO_ARRAYS:]
    enter_halo, refs = refs[0], refs[1:]
    (
        gain, state, shares,
        gains, got_core, half_total, got_pair, plane, chain_in, chain_out, pair_in, pair_out, core_out,
        gain_send, gain_recv, core_send, core_recv, pair_send, pair_recv,
        chain_send, chain_recv, back_send, back_recv, last_send, last_recv, halo_send, halo_recv,
        enter_send, enter_recv,
    ) = refs
    me = lax.axis_index("rows")
    c, x, z = me % 2, (me // 2) % 2, me // 4
    depth = count // 4
    core_peer = me + 1 - 2 * c
    pair_peer = me + 2 - 4 * x
    cross_peer = core_peer + 2 - 4 * x
    dirs = gain.shape[0]
    size = dirs // chunks
    peers = (core_peer, pair_peer, cross_peer)

    def part(j):
        return pl.ds(j * size, size)

    barrier = pltpu.get_barrier_semaphore()
    for peer in peers:
        pl.semaphore_signal(barrier, inc=1, device_id={"rows": peer}, device_id_type=MESH)

    @pl.when(z > 0)
    def _():
        pl.semaphore_signal(barrier, inc=1, device_id={"rows": me - 4}, device_id_type=MESH)

    @pl.when(z < depth - 1)
    def _():
        pl.semaphore_signal(barrier, inc=1, device_id={"rows": me + 4}, device_id_type=MESH)

    mine = lax.axis_index("dirs")
    higher, lower = (mine + 1) % dir_count, (mine + dir_count - 1) % dir_count
    neighbours = (higher, lower) if dir_count > 2 else (higher,)
    for peer in neighbours:
        pl.semaphore_signal(barrier, inc=1, device_id={"dirs": peer}, device_id_type=MESH)
    pl.semaphore_wait(
        barrier, 3 + len(neighbours) + (z > 0).astype(jnp.int32) + (z < depth - 1).astype(jnp.int32)
    )

    def remote(src, dst, send, recv, peer):
        return pltpu.make_async_remote_copy(
            src_ref=src, dst_ref=dst, send_sem=send, recv_sem=recv,
            device_id={"rows": peer}, device_id_type=MESH,
        )

    gain_copies = [
        remote(gain, gains.at[i], gain_send.at[i], gain_recv.at[i], peer) for i, peer in enumerate(peers)
    ]
    core_copies = [
        remote(state.at[1 - c, :, part(j)], got_core.at[:, part(j)], core_send.at[j], core_recv.at[j], core_peer)
        for j in range(chunks)
    ]
    pair_copies = [
        remote(half_total.at[1 - x, part(j)], got_pair.at[part(j)], pair_send.at[j], pair_recv.at[j], pair_peer)
        for j in range(chunks)
    ]
    back_copies = [
        remote(pair_out.at[part(j)], pair_in.at[x, part(j)], back_send.at[j], back_recv.at[j], pair_peer)
        for j in range(chunks)
    ]
    last_copies = [
        remote(core_out.at[:, part(j)], out.at[c, :, part(j)], last_send.at[j], last_recv.at[j], core_peer)
        for j in range(chunks)
    ]

    halo_copies, enter_copies = [], []
    for way, (peer, start, to) in enumerate(((lower, 0, SHIFT), (higher, dirs - SHIFT, 0))):
        enter_copies.append(
            pltpu.make_async_remote_copy(
                src_ref=out.at[:, :, pl.ds(start, SHIFT)], dst_ref=enter_halo.at[:, :, pl.ds(to, SHIFT)],
                send_sem=enter_send.at[way], recv_sem=enter_recv.at[way],
                device_id={"dirs": peer}, device_id_type=MESH,
            )
        )
        for i, array in enumerate(shared):
            halo_copies.append(
                pltpu.make_async_remote_copy(
                    src_ref=array.at[pl.ds(start, SHIFT)], dst_ref=halos[i].at[pl.ds(to, SHIFT)],
                    send_sem=halo_send.at[way, i], recv_sem=halo_recv.at[way, i],
                    device_id={"dirs": peer}, device_id_type=MESH,
                )
            )
            halo_copies[-1].start()

    flags = marks[:, 1:2, :]
    flags = flags - 2.0 * jnp.floor(0.5 * flags)
    back = jnp.concatenate([flags] * (gain.shape[-1] // flags.shape[-1]), axis=2)
    sea = sea_mask[...].astype(f32)
    for d in range(dirs):
        onward, onward_gain = row_weights(coupling[d], sea, False)
        against, _ = row_weights(coupling[d], sea, True)
        shares[d] = jnp.where(back[d] > 0.5, against, onward)
        gain[d] = onward_gain
    for copy in gain_copies:
        copy.start()
    order = [0] + list(range(chunks - 1, 0, -1))
    for j in order:

        def compose(d, _):
            share = shares[d]
            for h in range(2):
                for q in range(2):
                    band = (2 * h + q) * state.shape[3]
                    values = previous[d, band : band + state.shape[3]].astype(f32)
                    state[h, q, d] = jnp.sum(values * share[None], axis=1)
            return 0

        lax.fori_loop(j * size, (j + 1) * size, compose, 0)
        core_copies[j].start()
    c_bit, x_bit = c.astype(f32), x.astype(f32)
    core_after = c_bit + back - 2.0 * c_bit * back
    pair_after = x_bit + back - 2.0 * x_bit * back
    for copy in gain_copies:
        copy.wait_recv()
    core_mine, core_theirs = gain[...], gains[0]
    pair_mine, pair_theirs = core_mine * core_theirs, gains[1] * gains[2]
    plane_gain = pair_mine * pair_theirs

    def total(after, mine, theirs):
        return after * mine + (1.0 - after), (1.0 - after) * theirs + after

    core_a, core_b = total(core_after, core_mine, core_theirs)
    pair_a, pair_b = total(pair_after, pair_mine, pair_theirs)

    def cut(v, j):
        return v[j * size : (j + 1) * size]

    for j in order:
        core_copies[j].wait_recv()
        half_total[:, part(j)] = (
            cut(core_a, j)[None] * got_core[:, part(j)] + cut(core_b, j)[None] * state[c, :, part(j)]
        )
        pair_copies[j].start()
    for j in order:
        pair_copies[j].wait_recv()
        plane[part(j)] = cut(pair_a, j) * got_pair[part(j)] + cut(pair_b, j) * half_total[x, part(j)]

    upper = (2 * z >= depth).astype(jnp.int32)
    mine_at = 2 * c + x

    def chain(j, way):
        step = 1 - 2 * way
        has_before = jnp.where(way == 0, z > 0, z < depth - 1)
        has_after = jnp.where(way == 0, z < depth - 1, z > 0)
        copy = remote(
            chain_out.at[way, part(j)], chain_in.at[way, part(j)],
            chain_send.at[way, j], chain_recv.at[way, j], me + 4 * step,
        )

        @pl.when(has_before)
        def _():
            copy.wait_recv()

        @pl.when(jnp.logical_not(has_before))
        def _():
            chain_in[way, part(j)] = boundary[part(j), mine_at]

        @pl.when(has_after)
        def _():
            chain_out[way, part(j)] = cut(plane_gain, j) * chain_in[way, part(j)] + plane[part(j)]
            copy.start()

    def split(after, mine, theirs):
        return after * theirs + (1.0 - after), (1.0 - after) * mine + after

    pair_p, pair_q = split(pair_after, pair_mine, pair_theirs)
    core_p, core_q = split(core_after, core_mine, core_theirs)
    for j in order:
        chain(j, upper)
        chain(j, 1 - upper)
        entering = jnp.where(cut(back, j) > 0.5, chain_in[1, part(j)], chain_in[0, part(j)])
        pair_out[part(j)] = cut(pair_q, j) * entering + (1.0 - cut(pair_after, j)) * half_total[x, part(j)]
        back_copies[j].start()
        pair_in[x, part(j)] = cut(pair_p, j) * entering + cut(pair_after, j) * got_pair[part(j)]
    for j in order:
        back_copies[j].wait_recv()
        entering = pair_in[:, part(j)]
        core_out[:, part(j)] = (
            cut(core_q, j)[None] * entering + (1.0 - cut(core_after, j))[None] * state[c, :, part(j)]
        )
        last_copies[j].start()
        out[c, :, part(j)] = cut(core_p, j)[None] * entering + cut(core_after, j)[None] * got_core[:, part(j)]
    for j in order:
        last_copies[j].wait_recv()
        if j == 0:
            enter_copies[0].start()
        if j == chunks - 1:
            enter_copies[1].start()
    for copy in halo_copies + enter_copies:
        copy.wait_recv()
    for copy in halo_copies + enter_copies + gain_copies + core_copies + pair_copies + back_copies + last_copies:
        copy.wait_send()

    def drain(j, way):
        copy = remote(
            chain_out.at[way, part(j)], chain_in.at[way, part(j)],
            chain_send.at[way, j], chain_recv.at[way, j], me + 4 * (1 - 2 * way),
        )

        @pl.when(z < depth - 1 if way == 0 else z > 0)
        def _():
            copy.wait_send()

    for j in range(chunks):
        drain(j, 0)
        drain(j, 1)


def scan_devices(count, dir_count, boundary, sea_mask, previous, coupling, inverse, marks):
    dirs, bands, _, columns = previous.shape
    chunks = 1
    quarter = bands // 4
    boundary = boundary.reshape(dirs, 4, quarter, columns)
    vmem = pl.BlockSpec(memory_space=pltpu.VMEM)
    part = (dirs, quarter, columns)
    dma = pltpu.SemaphoreType.DMA
    anywhere = pl.BlockSpec(memory_space=pl.ANY)
    shared = (previous, coupling, inverse, marks)
    halos = [jax.ShapeDtypeStruct((2 * SHIFT,) + a.shape[1:], a.dtype) for a in shared]
    out, *halos = pl.pallas_call(
        functools.partial(scan_kernel, count, dir_count, chunks),
        in_specs=[vmem, vmem, vmem, vmem, anywhere, vmem],
        out_specs=[vmem] + [anywhere] * HALO_ARRAYS + [vmem],
        out_shape=[jax.ShapeDtypeStruct((2, 2) + part, f32)]
        + halos
        + [jax.ShapeDtypeStruct((2, 2, 2 * SHIFT, quarter, columns), f32)],
        scratch_shapes=[
            pltpu.VMEM((dirs, 1, columns), f32),
            pltpu.VMEM((2, 2) + part, f32),
            pltpu.VMEM(coupling.shape, f32),
            pltpu.VMEM((3, dirs, 1, columns), f32),
            pltpu.VMEM((2,) + part, f32),
            pltpu.VMEM((2,) + part, f32),
            pltpu.VMEM(part, f32),
            pltpu.VMEM(part, f32),
            pltpu.VMEM((2,) + part, f32),
            pltpu.VMEM((2,) + part, f32),
            pltpu.VMEM((2,) + part, f32),
            pltpu.VMEM(part, f32),
            pltpu.VMEM((2,) + part, f32),
            dma((3,)), dma((3,)),
            dma((chunks,)), dma((chunks,)),
            dma((chunks,)), dma((chunks,)),
            dma((2, chunks)), dma((2, chunks)),
            dma((chunks,)), dma((chunks,)),
            dma((chunks,)), dma((chunks,)),
            dma((2, HALO_ARRAYS)), dma((2, HALO_ARRAYS)),
            dma((2,)), dma((2,)),
        ],
        compiler_params=pltpu.CompilerParams(
            collective_id=0, has_side_effects=True, vmem_limit_bytes=VMEM_BYTES
        ),
        cost_estimate=cost(35),
        name="scan_devices",
    )(boundary, sea_mask, previous, coupling, inverse, marks)
    return (
        out.reshape(4, dirs, quarter, columns),
        halos[:HALO_ARRAYS],
        halos[HALO_ARRAYS].reshape(4, 2 * SHIFT, quarter, columns),
    )


def step_kernel(
    dirs, quadrant, cross_gain, halo_marks, coef, sea_mask, wet_tiles,
    previous, coupling, inverse, entering,
    halo_previous, halo_coupling, halo_inverse, halo_entering,
    out, swept, rounded, settled, sea, wet,
):
    t = pl.program_id(0)
    _, bands, rows, columns = previous.shape
    block = inverse.shape[-1]
    pieces = columns // block
    quarter = bands // 4

    @pl.when(t == 0)
    def _():
        sea[...] = sea_mask[...].astype(f32)
        for k in range(pieces):
            flag = wet_tiles[:, k : k + 1].astype(f32)
            wet[:, k * block : (k + 1) * block] = jnp.broadcast_to(flag, (rows, block))

    def sweep(previous, coupling, entering, backward):
        couple, weight = weights(coupling[0], sea[...])
        order = visit_order(couple.shape, backward)
        first = jnp.where(order == 0, couple, 0.0)
        spans, reach, span = [], couple, 1
        while span < rows:
            spans.append((span, jnp.where(order >= span, reach, 0.0)))
            reach = jnp.where(order >= span, reach * rolled(reach, span, backward), reach)
            span *= 2

        def group(q, _):
            inflow = entering[q, 0]
            for r in range(quarter):
                value = weight * previous[0, q * quarter + r].astype(f32) + first * inflow[r : r + 1]
                for span, factor in spans:
                    value = value + factor * rolled(value, span, backward)
                swept[q * quarter + r] = value
            return 0

        lax.fori_loop(0, 4, group, 0)

    def columns_solve(inverse, gain, slot, keep, sideways):
        matrix = inverse[0] if sideways else inverse[0].T
        carry = gain * (matrix[block - 1 :] if sideways else matrix[:1])
        high = matrix.astype(bf16)
        low = (matrix - high.astype(f32)).astype(bf16)
        whole = jnp.concatenate(
            [
                jnp.concatenate([high, low], axis=1),
                jnp.concatenate([high, jnp.zeros_like(low)], axis=1),
            ],
            axis=0,
        )
        before = None
        for k in range(pieces - 1, -1, -1) if sideways else range(pieces):
            here = slice(k * block, (k + 1) * block)
            x = swept[:, :, here].reshape(bands * rows, block)
            upper = x.astype(bf16)
            lower = (x - upper.astype(f32)).astype(bf16)
            both = jnp.dot(
                jnp.concatenate([upper, lower], axis=1), whole, preferred_element_type=f32
            )
            y = both[:, :block] + both[:, block:]
            if before is not None:
                y = y + (before[:, :1] if sideways else before[:, block - 1 :]) * carry
            before = y
            masked = y.reshape(bands, rows, block) * sea[:, here][None]
            rounded[slot, :, :, here] = masked.astype(bf16)
            if keep:
                settled[t, :, :, here] = masked

    def settle(previous, coupling, inverse, entering, corner, gain, slot, keep):
        for flag in (0, 1):
            pl.when(corner % 2 == flag)(
                functools.partial(sweep, previous, coupling, entering, flag == 1)
            )
        for flag in (0, 1):
            pl.when(corner // 2 == flag)(
                functools.partial(columns_solve, inverse, gain, slot, keep, flag == 1)
            )

    @pl.when(t < dirs)
    def _():
        at = jnp.minimum(t, dirs - 1)
        settle(previous, coupling, inverse, entering, quadrant[at], cross_gain[at], t + SHIFT, True)

    @pl.when(t >= dirs)
    def _():
        at = jnp.maximum(t - dirs, 0)
        settle(
            halo_previous, halo_coupling, halo_inverse, halo_entering,
            halo_marks[at, 1, 0].astype(jnp.int32), halo_marks[at, 0, 0],
            jnp.where(t < dirs + SHIFT, t - dirs, t), False,
        )

    @pl.when((t >= dirs) | (t >= 2 * SHIFT))
    def _():
        d = source_place(dirs, t)
        wet_cells = wet[...]

        def one(f, onward, against):
            energy = rounded[d + SHIFT, f].astype(f32)
            source = coef[f] * (
                energy * energy * (onward + against) - 2.0 * energy * onward * against
            )
            out[0, f] = (settled[d, f] + wet_cells * source.astype(bf16).astype(f32)).astype(bf16)

        def above(f):
            return rounded[d + 2 * SHIFT, f + 1].astype(f32)

        def below(f):
            return rounded[d, f - 1].astype(f32)

        nothing = jnp.zeros(wet.shape, f32)
        one(0, above(0), nothing)
        one(bands - 1, nothing, below(bands - 1))

        def body(f, _):
            one(f, above(f), below(f))
            return 0

        lax.fori_loop(1, bands - 1, body, 0, unroll=6 if (bands - 2) % 6 == 0 else 1)


def source_place(dirs, t):
    inner = jnp.clip(t - SHIFT, SHIFT, dirs - SHIFT - 1) if dirs > 2 * SHIFT else 0
    edge = jnp.where(t < dirs + SHIFT, t - dirs, t - 2 * SHIFT)
    return jnp.where(t < dirs, inner, edge)


def add_step(
    quadrant, cross_gain, quad_coef, sea_mask, wet_tiles,
    previous, coupling, inverse, entering, halos, halo_entering,
):
    dirs, bands, rows, columns = previous.shape
    halo_previous, halo_coupling, halo_inverse, halo_marks = halos
    smem = pl.BlockSpec(memory_space=pltpu.SMEM)

    def own(t):
        return jnp.minimum(t, dirs - 1)

    def halo(t):
        return jnp.maximum(t - dirs, 0)

    def specs(at):
        return [
            pl.BlockSpec((1,) + previous.shape[1:], lambda t: (at(t), 0, 0, 0)),
            pl.BlockSpec((1,) + coupling.shape[1:], lambda t: (at(t), 0, 0)),
            pl.BlockSpec((1,) + inverse.shape[1:], lambda t: (at(t), 0, 0)),
            pl.BlockSpec((4, 1) + entering.shape[2:], lambda t: (0, at(t), 0, 0)),
        ]

    return pl.pallas_call(
        functools.partial(step_kernel, dirs),
        grid=(dirs + 2 * SHIFT,),
        in_specs=[
            smem, smem, smem, smem,
            pl.BlockSpec(sea_mask.shape, lambda t: (0, 0)),
            pl.BlockSpec(wet_tiles.shape, lambda t: (0, 0)),
        ]
        + specs(own)
        + specs(halo),
        out_specs=pl.BlockSpec(
            (1,) + previous.shape[1:], lambda t: (source_place(dirs, t), 0, 0, 0)
        ),
        out_shape=jax.ShapeDtypeStruct(previous.shape, bf16),
        scratch_shapes=[
            pltpu.VMEM((bands, rows, columns), f32),
            pltpu.VMEM((dirs + 2 * SHIFT, bands, rows, columns), bf16),
            pltpu.VMEM((dirs, bands, rows, columns), f32),
            pltpu.VMEM((rows, columns), f32),
            pltpu.VMEM((rows, columns), f32),
        ],
        compiler_params=pltpu.CompilerParams(vmem_limit_bytes=VMEM_BYTES),
        cost_estimate=cost(20),
        name="add_step",
    )(
        quadrant, cross_gain, halo_marks, quad_coef, sea_mask, wet_tiles,
        previous, coupling, inverse, entering,
        halo_previous, halo_coupling, halo_inverse, halo_entering,
    )


def on_device(
    row_devices, dir_devices,
    previous, boundary, row_coupling, cross_gain, block_inverse, quadrant, sea_mask, wet_tiles, quad_coef,
):
    dirs = previous.shape[0]
    block = block_inverse.shape[-1]
    marks = jnp.broadcast_to(
        jnp.stack([cross_gain, quadrant.astype(f32)], 1)[:, :, None], (dirs, 2, block)
    )
    entering, halos, halo_entering = scan_devices(
        row_devices, dir_devices, boundary, sea_mask, previous, row_coupling, block_inverse, marks
    )
    return add_step(
        quadrant, cross_gain, quad_coef, sea_mask, wet_tiles,
        previous, row_coupling, block_inverse, entering, halos, halo_entering,
    )


def solution(mesh):
    in_specs = (
        P("dirs", None, "rows", None),
        P("dirs", None, None),
        P("dirs", "rows", None),
        P("dirs"),
        P("dirs", None, None),
        P("dirs"),
        P("rows", None),
        P("rows", None),
        P(),
    )
    out_specs = P("dirs", None, "rows", None)
    return jax.shard_map(
        functools.partial(on_device, mesh.shape["rows"], mesh.shape["dirs"]),
        mesh=mesh, in_specs=in_specs, out_specs=out_specs, check_vma=False,
    )
```

time: 97.4 us -> 72.4 us (0.74)
  Pallas kernels: 85 us -> 65.4 us
  other arithmetic: 5.45 us -> 1.39 us
  starting transfers between devices: 2.09 us -> 0 us
  local copies, waits for them, and re-layouts: 3.56 us -> 4.85 us
    pallas_call x5 -> x1, Pallas kernels: 36.2 us -> 19.8 us  [add_step(): pl.pallas_call(functools.partial(step_kernel, dirs), grid=(dirs + 2 * SHI...]
    convert_element_type x5 -> x0, other arithmetic: 3.7 us -> none  [the longest x1 1.48 us: on_device(): high = high.astype(bf16)]
    pallas_call x1, Pallas kernels: 48.8 us -> 45.7 us  [scan_devices(): pl.pallas_call(functools.partial(scan_kernel, count, dir_count, chunks),...]
    ppermute x2 -> x0, starting transfers between devices: 2.09 us -> none  [the longest x1 1.51 us: from_above(): return lax.ppermute(a, 'dirs', down)]
    unnamed x19 -> x17, local copies, waits for them, and re-layouts: 3.29 us -> 4.68 us
    another operation x0 -> x2, other arithmetic: none -> 1.39 us  [on_device(): jnp.stack([cross_gain, quadrant.astype(f32)], 1)[:, :, None]]
  transfers between devices with their start and end apart: 2 -> 0, of which waited for: 0 -> 0; matrix products, arithmetic and copies ran while one was open for 0% -> 0% of each run, Pallas kernels for 16% -> 0%
where the time goes in v2:
time: 72.4 us; the launch traced here: 71.7 us
  Pallas kernels  65.4 us (90%)
  local copies, waits for them, and re-layouts  4.85 us (7%)
  other arithmetic  1.39 us (2%)
    pallas_call x1, Pallas kernels, scan_devices(): pl.pallas_call(functools.partial(scan_kernel, count, dir_count, chunks),...  45.7 us
    pallas_call x1, Pallas kernels, add_step(): pl.pallas_call(functools.partial(step_kernel, dirs), grid=(dirs + 2 * SHI...  19.8 us
    unnamed x17, local copies, waits for them, and re-layouts  4.68 us

profile of v2, /device:TPU:0, one launch (start us, length us, event | category | flops | bytes accessed | tf_op | source)
XLA Modules:
  0.0 71.7 jit_solution(18315618695728713729)
XLA Ops:
  0.0 0.0 copy-start.6
  0.0 0.0 copy-start.5
  0.0 0.0 copy-start.7
  0.0 0.7 %convert_bitcast_fusion = f32[12,1]{0,1:T(1,128)S(1)} fusion(s32[12]{0:T(128)} %quadrant.1), kind=kLoop, calls=%fused_computation.1 | loop fusion | flops 12 | bytes 96 | tf_op jit(solution)/shard_map/stack | solution.py:512
  0.7 0.7 pad_maximum_fusion
  1.4 0.8 %copy.11.wet_tiles = s32[8,4]{1,0:T(8,128)S(1)} copy(s32[8,4]{0,1:T(4,128)} %param.16) | data formatting | bytes 256 | tf_op args[7]
  2.2 0.1 copy.10
  2.2 0.1 broadcast_in_dim.2.marks
  2.3 0.0 copy-start
  2.3 1.1 %copy-done = f32[12,128,128]{2,1,0:T(8,128)S(1)} copy-done((f32[12,128,128]{2,1,0:T(8,128)S(1)}, f32[12,128,128]{2,1,0:T(8,128)}, u32[]{:S(2)}) %copy-start) | copy-done | bytes 786456
  3.5 0.0 copy-start.2
  3.5 0.9 %copy-done.2 = f32[12,8,512]{2,1,0:T(8,128)S(1)} copy-done((f32[12,8,512]{2,1,0:T(8,128)S(1)}, f32[12,8,512]{2,1,0:T(8,128)}, u32[]{:S(2)}) %copy-start.2) | copy-done | bytes 196632
  4.4 0.0 copy-start.3
  4.4 1.1 %copy-done.3 = f32[12,32,512]{2,1,0:T(8,128)S(1)} copy-done((f32[12,32,512]{2,1,0:T(8,128)S(1)}, f32[12,32,512]{2,1,0:T(8,128)}, u32[]{:S(2)}) %copy-start.3) | copy-done | bytes 786456
  5.5 0.0 copy-start.4
  5.5 0.7 copy-done.4
  6.2 0.0 copy-start.1
  6.2 45.7 %scan_devices.1 = (f32[2,2,12,8,512]{4,3,2,1,0:T(8,128)S(1)}, bf16[4,32,8,512]{3,2,1,0:T(8,128)(2,1)S(1)}, f32[4,8,512]{2,1,0:T(8,128)S(1)}, f32[4,128,128]{2,1,...) custom-call(f32[12,4,8,512]{3,2,1,0:T(8,128)S(1)} %bitcast.7, s32[8,512]{1,0:T(8,128)S(1)} %copy-done.4, ...), custom_call_target="tpu_custom_call" | custom-call | bytes 105000000 | tf_op jit(solution)/shard_map/scan_devices/pallas_call | solution.py:280
  51.9 0.0 copy-done.6
  51.9 0.0 copy-done.5
  51.9 0.0 copy-done.7
  51.9 0.0 copy-done.1
  52.0 19.8 %add_step.1 = bf16[12,32,8,512]{3,2,1,0:T(8,128)(2,1)} custom-call(s32[12]{0:T(128)S(1)} %copy-done.6, f32[12]{0:T(128)S(1)} %copy-done.5, f32[4,2,128]{2,1,0:T(2,128)S(1)} %get-tuple-element.11.halo_marks, f32[32]{0:T(128)S(1)} %copy-done.7, s32[8,512]{1,0:T(8,128)S(1)} %copy-done.4, s32[8,4]{1,0:T(8,128)S(1)} %copy.11.wet_tiles, ...), custom_call_target="tpu_custom_call" | custom-call | bytes 60000000 | tf_op jit(solution)/shard_map/add_step/pallas_call | solution.py:474
Async XLA Ops:
  0.0 51.9 %copy-start.6 = (s32[12]{0:T(128)S(1)}, s32[12]{0:T(128)}, u32[]{:S(2)}) copy-start(s32[12]{0:T(128)} %quadrant.1) | copy-start | bytes 148
  0.0 51.9 %copy-start.5 = (f32[12]{0:T(128)S(1)}, f32[12]{0:T(128)}, u32[]{:S(2)}) copy-start(f32[12]{0:T(128)} %cross_gain.1) | copy-start | bytes 148
  0.0 51.9 %copy-start.7 = (f32[32]{0:T(128)S(1)}, f32[32]{0:T(128)}, u32[]{:S(2)}) copy-start(f32[32]{0:T(128)} %coef.1) | copy-start | bytes 388
  2.3 1.1 %copy-start = (f32[12,128,128]{2,1,0:T(8,128)S(1)}, f32[12,128,128]{2,1,0:T(8,128)}, u32[]{:S(2)}) copy-start(f32[12,128,128]{2,1,0:T(8,128)} %inverse.3) | copy-start | bytes 2359300
  3.5 0.9 %copy-start.2 = (f32[12,8,512]{2,1,0:T(8,128)S(1)}, f32[12,8,512]{2,1,0:T(8,128)}, u32[]{:S(2)}) copy-start(f32[12,8,512]{2,1,0:T(8,128)} %coupling.3) | copy-start | bytes 589828
  4.4 1.1 %copy-start.3 = (f32[12,32,512]{2,1,0:T(8,128)S(1)}, f32[12,32,512]{2,1,0:T(8,128)}, u32[]{:S(2)}) copy-start(f32[12,32,512]{2,1,0:T(8,128)} %param.10) | copy-start | bytes 2359300
  5.5 0.7 %copy-start.4 = (s32[8,512]{1,0:T(8,128)S(1)}, s32[8,512]{1,0:T(8,128)}, u32[]{:S(2)}) copy-start(s32[8,512]{1,0:T(8,128)} %sea_mask.3) | copy-start | bytes 49156
  6.2 45.7 %copy-start.1 = (f32[12,128,128]{2,1,0:T(8,128)S(1)}, f32[12,128,128]{2,1,0:T(8,128)}, u32[]{:S(2)}) copy-start(f32[12,128,128]{2,1,0:T(8,128)} %inverse.3) | copy-start | bytes 2359300
